TPU v7x, 128 devices: a whole 4x4x4 slice. The times are simulated.
128 devices in a mesh: sec: 4 (over y_lo, core), tile: 32 (over y_hi, x, z).
Axes of the slice: x: 4, y: 4 (y_hi: 2, y_lo: 2; y = y_hi * 2 + y_lo), z: 4, core: 2. Of those that a mesh axis runs over, the one named last changes fastest.
Arguments:
- adjoint: float32 [4, 64, 256, 1024], P(None, None, 'tile', 'sec'), may hold values from -6 to 6
- kappa: float32 [63, 256, 1024], P(None, 'tile', 'sec'), may hold values from 0.1 to 600
- diffusion: float32 [256, 1024], P('tile', 'sec'), may hold values from 0.02 to 0.2
- gain: float32 [4], replicated, may hold values from 0.3 to 0.8
- store: bfloat16 [4, 1024, 4, 64, 256], P('sec', 'tile'), may hold values from -2.5 to 2.5
- sources: int32 [4, 256], P('sec'), may hold values from 0 to 1023, as said below
- ocean_mask: int32 [256, 256], P('tile'), may hold values 0 or 1
- remap: int32 [256, 256], P('tile'), may hold values from 0 to 6143, as said below
Outputs:
- result: float32 [4, 64, 256, 1024], P(None, None, 'tile', 'sec')
Inputs may be any that keep to these rules, and one draw needn't show every extreme that they name: sources[s, d * 8 + j] // 32 is the tile index, in sec row s, of the device that holds reader (s, d)'s trajectory block j, and sources % 32 its slot there. Each holder that a reader uses gives it exactly 2 of its 8 blocks. remap[R, i] = k * 8 * 256 + r * 256 + c: the atmosphere cell at row r of the same tile's rows and column c of atmosphere section k + 1.
All inputs are finite; a program needn't handle non-finite values. No bound on the sum of `ocean_mask` on one device may be relied on, other than what follows from the above.
Results may differ from a plain program's by a relative error of at most 0.0006.
Values may be sent and summed in bfloat16 or wider, within the bound.
A program may use at most 128 MiB of HBM per device.

v0:
```python
import functools

import jax
import jax.numpy as jnp
from jax import lax
from jax.experimental import pallas as pl
from jax.experimental.pallas import tpu as pltpu
from jax.sharding import PartitionSpec as P

F = 4
LEV = 64
ROWS = 8
LON = 256
NB = 8
SLOTS = 32
PLANE = LEV * ROWS
SIZE = {"y": 2, "x": 4, "z": 4}
ORDERS = (("x", "z", "y"), ("z", "y", "x"), ("y", "x", "z"))
PART_ROWS = (32, 48, 48)
PART_AT = (0, 32, 80)
MESH = pl.DeviceIdType.MESH
BF = jnp.bfloat16
F32 = jnp.float32
NT = (((1,), (1,)), ((), ()))
TN = (((0,), (0,)), ((), ()))


def coords(tile):
    return {"y": tile // 16, "x": (tile // 4) % 4, "z": tile % 4}


def tile_of(at):
    return at["y"] * 16 + at["x"] * 4 + at["z"]


def moved(at, axis, by):
    other = dict(at)
    other[axis] = lax.rem(at[axis] + by, SIZE[axis])
    return other


def rows_of(level):
    return pl.ds(pl.multiple_of(level * ROWS, ROWS), ROWS)


def wide(ref, at):
    return jnp.concatenate([ref[0, at, :], ref[1, at, :]], 1)


def put(ref, at, value):
    ref[0, at, :] = value[:, :128]
    ref[1, at, :] = value[:, 128:]


def kernel(adj, kappa, diff, store, mask, remap, gain, sources, out, *scratch):
    (store_v, st, mx, kap, inv, low, up, vel, diff_v, mask_v, remap_v, coef, dedge, cpl,
     s1, r1, r2, s3, r3, surf_s, surf_r, ew_s, ew_r, zw_s, zw_r, mr_s, mr_r, vr_s, vr_r,
     load_sem, out_sem, own_sem, e_send, e_recv, h_send, h_recv) = scratch
    tile = lax.axis_index("tile")
    sec = lax.axis_index("sec")
    me = coords(tile)

    loads = [
        pltpu.make_async_copy(adj.at[:, pl.ds(0, 128)], st.at[0], load_sem.at[0]),
        pltpu.make_async_copy(adj.at[:, pl.ds(128, 128)], st.at[1], load_sem.at[6]),
        pltpu.make_async_copy(store, store_v, load_sem.at[1]),
        pltpu.make_async_copy(kappa, kap.at[pl.ds(0, PLANE - ROWS)], load_sem.at[2]),
        pltpu.make_async_copy(diff, diff_v, load_sem.at[3]),
        pltpu.make_async_copy(mask, mask_v, load_sem.at[4]),
        pltpu.make_async_copy(remap, remap_v, load_sem.at[5]),
    ]
    for load in loads:
        load.start()

    barrier = pltpu.get_barrier_semaphore()
    greeted = 0
    for axis in ("x", "z", "y"):
        for by in range(1, SIZE[axis]):
            pl.semaphore_signal(barrier, inc=1, device_id={"tile": tile_of(moved(me, axis, by))},
                                device_id_type=MESH)
            greeted += 1
    for by in (1, 31):
        pl.semaphore_signal(barrier, inc=1, device_id={"tile": lax.rem(tile + by, 32)},
                            device_id_type=MESH)
        greeted += 1
    for by in (1, 2, 3):
        pl.semaphore_signal(barrier, inc=1, device_id={"sec": lax.rem(sec + by, 4)},
                            device_id_type=MESH)
        greeted += 1
    pl.semaphore_wait(barrier, greeted)

    pending = []
    arrivals = {}

    def send(key, src, dst, send_sem, recv_sem, device):
        copy = pltpu.make_async_remote_copy(src, dst, send_sem, recv_sem, device_id=device,
                                            device_id_type=MESH)
        copy.start()
        pending.append(copy)
        arrivals.setdefault(key, []).append(copy)

    def arrived(key):
        for copy in arrivals.pop(key):
            copy.wait_recv()

    hsem = [0]

    def small(key, src, dst, device):
        n = hsem[0]
        hsem[0] += 1
        send(key, src, dst, h_send.at[n], h_recv.at[n], device)

    def to_sections(key, src, dst):
        for by in (1, 2, 3):
            small(key, src, dst.at[sec], {"sec": lax.rem(sec + by, 4)})

    def to_north_south(key, src, dst):
        small(key, src.at[0], dst.at[0], {"tile": lax.rem(tile + 31, 32)})
        small(key, src.at[1], dst.at[1], {"tile": lax.rem(tile + 1, 32)})

    def esem(half, part, stage, by):
        return ((half * 3 + part) * 3 + stage) * 3 + by - 1

    def stage_one(half, part):
        a1, a2, a3 = ORDERS[part]
        n1, n2, n3 = SIZE[a1], SIZE[a2], SIZE[a3]
        rows = PART_ROWS[part]
        at = half * 128 + PART_AT[part]
        sbuf, rbuf = s1[half * 3 + part], r1[half * 3 + part]
        for by in list(range(1, n1)) + [0]:
            c1 = lax.rem(me[a1] + by, n1)

            def one_reader(i, _):
                c2, c3 = i // n3, lax.rem(i, n3)
                reader = tile_of({a1: c1, a2: c2, a3: c3})
                first = jnp.int32(0)
                second = jnp.int32(0)
                for j in range(NB):
                    source = sources[0, reader * NB + j]
                    mine = source // SLOTS == tile
                    second = jnp.where(mine, source % SLOTS, second)
                for j in reversed(range(NB)):
                    source = sources[0, reader * NB + j]
                    mine = source // SLOTS == tile
                    first = jnp.where(mine, source % SLOTS, first)
                for k, slot in ((0, first), (1, second)):
                    block = store_v[slot, at:at + rows, :]
                    if by:
                        sbuf[by - 1, c2, c3, k] = block
                    else:
                        rbuf[c2, me[a1], c3, k] = block
                return 0

            lax.fori_loop(0, n2 * n3, one_reader, 0)
            if by:
                n = esem(half, part, 0, by)
                send((half, part, 0), sbuf.at[by - 1], rbuf.at[:, me[a1]], e_send.at[n], e_recv.at[n],
                     {"tile": tile_of(moved(me, a1, by))})

    def stage_two(half, part):
        a1, a2, a3 = ORDERS[part]
        src, dst = r1[half * 3 + part], r2[half * 3 + part]
        arrived((half, part, 0))
        for by in range(1, SIZE[a2]):
            c2 = lax.rem(me[a2] + by, SIZE[a2])
            n = esem(half, part, 1, by)
            send((half, part, 1), src.at[c2], dst.at[me[a2]], e_send.at[n], e_recv.at[n],
                 {"tile": tile_of(moved(me, a2, by))})
        own = pltpu.make_async_copy(src.at[me[a2]], dst.at[me[a2]], own_sem.at[half * 3 + part])
        own.start()
        arrivals[("own", half, part)] = [own]

    def stage_three(half, part):
        a1, a2, a3 = ORDERS[part]
        n3 = SIZE[a3]
        src, sbuf, rbuf = r2[half * 3 + part], s3[half * 3 + part], r3[half * 3 + part]
        arrivals.pop(("own", half, part))[0].wait()
        arrived((half, part, 1))
        for by in list(range(1, n3)) + [0]:
            target = moved(me, a3, by)
            reader = tile_of(target)
            holders = [sources[0, reader * NB + j] // SLOTS for j in range(NB)]
            for j in range(NB):
                rank = jnp.int32(0)
                for i in range(j):
                    rank = rank + jnp.where(holders[i] == holders[j], 1, 0)
                holder = coords(holders[j])
                block = src[holder[a2], holder[a1], target[a3], jnp.minimum(rank, 1)]
                if by:
                    sbuf[by - 1, j] = block
                else:
                    rbuf[me[a3], j] = block
            if by:
                n = esem(half, part, 2, by)
                send((half, part, 2), sbuf.at[by - 1], rbuf.at[me[a3]], e_send.at[n], e_recv.at[n],
                     {"tile": reader})

    def assemble(half, part):
        a3 = ORDERS[part][2]
        arrived((half, part, 2))
        rows = PART_ROWS[part]
        for j in range(NB):
            holder = coords(sources[0, tile * NB + j] // SLOTS)
            block = r3[half * 3 + part][holder[a3], j]
            put(vel, pl.ds(PART_AT[part] * ROWS + j, rows, stride=ROWS), block.astype(F32))
            for side, edge in ((0, 0), (1, NB - 1)):
                if j == edge and part:
                    lo = max(PART_AT[part], LEV)
                    hi = PART_AT[part] + rows
                    vr_s[half][side, lo - LEV:hi - LEV, :] = block[lo - PART_AT[part]:]

    lane = lax.broadcasted_iota(jnp.int32, (ROWS, LON), 1)
    row = lax.broadcasted_iota(jnp.int32, (ROWS, LON), 0)

    def edge_pick(low_lane, high_lane, field=None):
        wanted = jnp.where(row % 2 == 0, low_lane, high_lane)
        pick = lane == wanted
        if field is not None:
            pick = pick & (row // 2 == field)
        return jnp.where(pick, 1.0, 0.0)

    def send_surface(step):
        for f in range(F):
            surf_s[step][pl.ds(f * ROWS, ROWS), :] = wide(st, pl.ds(f * PLANE, ROWS))
        to_sections(("surf", step), surf_s[step], surf_r[step])

    def prepare():
        kap[pl.ds(PLANE - ROWS, ROWS), :] = jnp.zeros((ROWS, LON), F32)

        def level(l, carry):
            g, below = carry
            at = rows_of(l)
            above = kap[at, :]
            p = 1.0 + below * g
            w = 1.0 / (p + above)
            inv[at, :] = w
            low[at, :] = below * w
            up[at, :] = above * w
            return p * w, above

        zero = jnp.zeros((ROWS, LON), F32)
        lax.fori_loop(0, LEV, level, (zero, zero))
        d = diff_v[...]
        is_ocean = sec == 0
        sea = jnp.where(is_ocean, mask_v[...].astype(F32), 1.0)
        east_ok = jnp.where(is_ocean | (lane != 0), 1.0, 0.0)
        west_ok = jnp.where(is_ocean | (lane != LON - 1), 1.0, 0.0)
        north_ok = jnp.where(row != 0, 1.0, 0.0)
        south_ok = jnp.where(row != ROWS - 1, 1.0, 0.0)
        coef[0] = pltpu.roll(d, 1, 1) * east_ok
        coef[1] = 0.5 * east_ok
        coef[2] = pltpu.roll(d, LON - 1, 1) * west_ok
        coef[3] = 0.5 * west_ok
        coef[4] = pltpu.roll(d, 1, 0) * north_ok
        coef[5] = 0.5 * north_ok
        coef[6] = pltpu.roll(d, ROWS - 1, 0) * south_ok
        coef[7] = 0.5 * south_ok
        coef[8] = 1.0 - 4.0 * d
        coef[9] = sea
        tiled = jnp.broadcast_to(d[None], (LEV, ROWS, LON)).reshape(PLANE, LON)
        dedge[...] = lax.dot_general(edge_pick(LON - 1, 0), tiled, NT,
                                     precision=lax.Precision.HIGHEST, preferred_element_type=F32)

    def couple(step):
        surf_r[step][sec] = surf_s[step][...]
        arrived(("surf", step))
        iota = lax.broadcasted_iota(jnp.int32, (128, LON), 0)

        def parts_of(r):
            cell = remap_v[r:r + 1, :]
            onehot = jnp.where(iota == (cell & 127), 1.0, 0.0).astype(BF)
            high = ((cell >> 11) << 4) + (((cell >> 7) & 1) << 3) + ((cell >> 8) & 7)
            return onehot, high, mask_v[r:r + 1, :].astype(F32)

        @pl.when(sec == 0)
        def _():
            table = jnp.concatenate(
                [surf_r[step][s + 1, f * ROWS:(f + 1) * ROWS, h * 128:(h + 1) * 128]
                 for f in range(F) for s in range(3) for h in range(2)], 0).astype(BF)
            iota48 = lax.broadcasted_iota(jnp.int32, (48, LON), 0)
            for r in range(ROWS):
                onehot, high, sea = parts_of(r)
                found = jnp.dot(table, onehot, preferred_element_type=F32)
                hit = iota48 == high
                for f in range(F):
                    value = jnp.sum(jnp.where(hit, found[f * 48:(f + 1) * 48], 0.0), 0, keepdims=True)
                    cpl[f * ROWS + r:f * ROWS + r + 1, :] = gain[f] * sea * value

        @pl.when(sec != 0)
        def _():
            iota16 = lax.broadcasted_iota(jnp.int32, (16, LON), 0)
            total = jnp.zeros((F * 16, 128), F32)
            for r in range(ROWS):
                onehot, high, sea = parts_of(r)
                hit = iota16 == high - (sec - 1) * 16
                spread = []
                for f in range(F):
                    value = gain[f] * sea * surf_r[step][0, f * ROWS + r:f * ROWS + r + 1, :]
                    spread.append(jnp.where(hit, value, 0.0))
                spread = jnp.concatenate(spread, 0).astype(BF)
                total = total + lax.dot_general(spread, onehot, NT, preferred_element_type=F32)
            for f in range(F):
                for h in range(2):
                    at = (f * 2 + h) * ROWS
                    cpl[f * ROWS:(f + 1) * ROWS, h * 128:(h + 1) * 128] = total[at:at + ROWS]

        for f in range(F):
            at = pl.ds(f * PLANE, ROWS)
            put(st, at, wide(st, at) + cpl[pl.ds(f * ROWS, ROWS), :])

    def solve():
        def forward(l, carry):
            at = rows_of(l)
            w, a = inv[at, :], low[at, :]
            result = []
            for f in range(F):
                here = rows_of(f * LEV + l)
                d = wide(st, here) * w + a * carry[f]
                put(mx, here, d)
                result.append(d)
            return tuple(result)

        def backward(i, carry):
            l = LEV - 1 - i
            e = up[rows_of(l), :]
            result = []
            for f in range(F):
                here = rows_of(f * LEV + l)
                x = wide(mx, here) + e * carry[f]
                put(mx, here, x)
                result.append(x)
            return tuple(result)

        zero = tuple(jnp.zeros((ROWS, LON), F32) for _ in range(F))
        lax.fori_loop(0, LEV, forward, zero)
        lax.fori_loop(0, LEV, backward, zero)

    def send_mixed(step):
        for side, edge in ((0, 0), (1, ROWS - 1)):
            for f in range(F):
                mr_s[step][side, f * LEV:(f + 1) * LEV, :] = wide(
                    mx, pl.ds(f * PLANE + edge, LEV, stride=ROWS)).astype(BF)
        to_north_south(("mr", step), mr_s[step], mr_r[step])
        total = jnp.zeros((ROWS, PLANE), F32)
        for f in range(F):
            total = total + lax.dot_general(
                edge_pick(0, LON - 1, f).astype(BF), wide(mx, pl.ds(f * PLANE, PLANE)).astype(BF), NT,
                preferred_element_type=F32)
        ew_s[step][...] = total
        to_sections(("ew", step), ew_s[step], ew_r[step])

    def send_velocity(step):
        to_north_south(("vr", step), vr_s[step], vr_r[step])
        zw_s[step][...] = lax.dot_general(edge_pick(0, LON - 1).astype(BF), wide(vel, pl.ds(0, PLANE)).astype(BF), NT,
                                          preferred_element_type=F32)
        to_sections(("zw", step), zw_s[step], zw_r[step])

    def stencil():
        def level(l, _):
            z = wide(vel, rows_of(l))
            v = wide(vel, rows_of(LEV + l))
            c_e = coef[0] + coef[1] * z
            c_w = coef[2] - coef[3] * z
            c_n = coef[4] + coef[5] * v
            c_s = coef[6] - coef[7] * v
            for f in range(F):
                here = rows_of(f * LEV + l)
                m = wide(mx, here)
                total = m * coef[8]
                total = total + pltpu.roll(m * c_e, LON - 1, 1)
                total = total + pltpu.roll(m * c_w, 1, 1)
                total = total + pltpu.roll(m * c_n, ROWS - 1, 0)
                total = total + pltpu.roll(m * c_s, 1, 0)
                put(st, here, total * coef[9])
            return 0

        lax.fori_loop(0, LEV, level, 0)

    def add_halos(step, done=None):
        arrived(("mr", step))
        arrived(("vr", step))
        arrived(("ew", step))
        arrived(("zw", step))
        even = lax.broadcasted_iota(jnp.int32, (ROWS, PLANE), 0) % 2 == 0
        east = jnp.where(sec >= 3, 1, sec + 1)
        west = jnp.where(sec <= 1, 3, sec - 1)
        m = jnp.where(even, ew_r[step][jnp.where(sec == 0, 1, east)], ew_r[step][jnp.where(sec == 0, 2, west)])
        z = jnp.where(even, zw_r[step][jnp.where(sec == 0, 1, east)],
                      -zw_r[step][jnp.where(sec == 0, 2, west)])
        value = jnp.where(sec == 0, 0.0, m * (dedge[...] + 0.5 * z)).astype(BF)
        for f in range(F):
            for side, edge, missing, sign in ((0, ROWS - 1, 31, 0.5), (1, 0, 0, -0.5)):
                rows = mr_r[step][side, f * LEV:(f + 1) * LEV, :].astype(F32)
                v = vr_r[step][side].astype(F32)
                term = rows * (diff_v[edge:edge + 1, :] + sign * v) * coef[9, edge:edge + 1, :]
                term = jnp.where(tile == missing, 0.0, term)
                at = pl.ds(f * PLANE + edge, LEV, stride=ROWS)
                put(st, at, wide(st, at) + term)

            @pl.when(sec != 0)
            def _():
                place = edge_pick(LON - 1, 0, f).astype(BF)
                at = pl.ds(f * PLANE, PLANE)
                put(st, at, wide(st, at) + lax.dot_general(value, place, TN, preferred_element_type=F32))

            if done is not None:
                done(f)

    def finish(f):
        at = pl.ds(f * PLANE, PLANE)
        for h in range(2):
            copy = pltpu.make_async_copy(st.at[h, at], out.at[at, pl.ds(h * 128, 128)], out_sem.at[f, h])
            copy.start()
            outs.append(copy)

    outs = []
    loads[0].wait()
    loads[1].wait()
    send_surface(0)
    loads[2].wait()
    for part in (2, 1, 0):
        stage_one(0, part)
    for part in (2, 1, 0):
        stage_one(1, part)
    for load in loads[3:]:
        load.wait()
    prepare()
    couple(0)
    solve()
    send_mixed(0)
    for part in (2, 1, 0):
        stage_two(0, part)
    for part in (0, 2, 1):
        stage_three(0, part)
    for part in (2, 1, 0):
        stage_two(1, part)
    for part in (0, 2, 1):
        assemble(0, part)
    send_velocity(0)
    stencil()
    add_halos(0)
    send_surface(1)
    for part in (0, 2, 1):
        stage_three(1, part)
    couple(1)
    solve()
    send_mixed(1)
    for part in (0, 2, 1):
        assemble(1, part)
    send_velocity(1)
    stencil()
    add_halos(1, finish)
    for copy in outs:
        copy.wait()
    for copy in pending:
        copy.wait_send()


def per_device(adjoint, kappa, diffusion, gain, store, sources, ocean_mask, remap):
    vmem, dma = pltpu.VMEM, pltpu.SemaphoreType.DMA
    both = range(2)

    def each(shape_of):
        return [vmem(shape_of(part), BF) for _ in both for part in range(3)]

    def sizes(part):
        return tuple(SIZE[a] for a in ORDERS[part])

    def s1_shape(part):
        n1, n2, n3 = sizes(part)
        return (n1 - 1, n2, n3, 2, PART_ROWS[part], LON)

    def r1_shape(part):
        n1, n2, n3 = sizes(part)
        return (n2, n1, n3, 2, PART_ROWS[part], LON)

    def s3_shape(part):
        return (sizes(part)[2] - 1, NB, PART_ROWS[part], LON)

    def r3_shape(part):
        return (sizes(part)[2], NB, PART_ROWS[part], LON)

    def twice(shape, kind):
        return [vmem(shape, kind) for _ in both]

    state = F * PLANE
    scratch = [
        vmem((SLOTS, F * LEV, LON), BF), vmem((2, state, 128), F32), vmem((2, state, 128), F32),
        vmem((PLANE, LON), F32), vmem((PLANE, LON), F32), vmem((PLANE, LON), F32), vmem((PLANE, LON), F32),
        vmem((2, 2 * PLANE, 128), F32), vmem((ROWS, LON), F32), vmem((ROWS, LON), jnp.int32),
        vmem((ROWS, LON), jnp.int32), vmem((10, ROWS, LON), F32), vmem((ROWS, PLANE), F32),
        vmem((F * ROWS, LON), F32),
        each(s1_shape), each(r1_shape), each(r1_shape), each(s3_shape), each(r3_shape),
        twice((F * ROWS, LON), F32), twice((4, F * ROWS, LON), F32),
        twice((ROWS, PLANE), F32), twice((4, ROWS, PLANE), F32),
        twice((ROWS, PLANE), F32), twice((4, ROWS, PLANE), F32),
        twice((2, F * LEV, LON), BF), twice((2, F * LEV, LON), BF),
        twice((2, LEV, LON), BF), twice((2, LEV, LON), BF),
        dma((7,)), dma((F, 2)), dma((6,)), dma((54,)), dma((54,)), dma((26,)), dma((26,)),
    ]
    leaves, tree = jax.tree.flatten(scratch)

    def body(*refs):
        head, rest = refs[:9], refs[9:]
        kernel(*head, *jax.tree.unflatten(tree, rest))

    anywhere = pl.BlockSpec(memory_space=pl.ANY)
    scalar = pl.BlockSpec(memory_space=pltpu.SMEM)
    result = pl.pallas_call(
        body,
        out_shape=jax.ShapeDtypeStruct((state, LON), F32),
        in_specs=[anywhere] * 6 + [scalar] * 2,
        out_specs=anywhere,
        scratch_shapes=leaves,
        compiler_params=pltpu.CompilerParams(
            collective_id=0, has_side_effects=True, vmem_limit_bytes=56 * 2**20
        ),
        cost_estimate=pl.CostEstimate(flops=100_000_000, bytes_accessed=10_000_000, transcendentals=0),
    )(
        adjoint.reshape(state, LON), kappa.reshape(PLANE - ROWS, LON), diffusion,
        store.reshape(SLOTS, F * LEV, LON), ocean_mask, remap, gain, sources,
    )
    return result.reshape(F, LEV, ROWS, LON)


def solution(mesh):
    return jax.shard_map(
        per_device,
        mesh=mesh,
        in_specs=(
            P(None, None, "tile", "sec"),
            P(None, "tile", "sec"),
            P("tile", "sec"),
            P(),
            P("sec", "tile", None, None, None),
            P("sec", None),
            P("tile", None),
            P("tile", None),
        ),
        out_specs=P(None, None, "tile", "sec"),
        check_vma=False,
    )
```

profile of v0, /device:TPU:1, one launch (start us, length us, event | category | flops | bytes accessed | tf_op | source)
XLA Modules:
  0.0 119.5 jit_solution(15329838823292054794)
XLA Ops:
  0.0 116.4 %shard_map.82 = f32[2048,256]{1,0:T(8,128)} custom-call(f32[2048,256]{1,0:T(8,128)} %bitcast.6, f32[504,256]{1,0:T(8,128)} %bitcast.7, f32[8,256]{1,0:T(8,128)} %refs_2_.1, bf16[32,256,256]{2,1,0:T(8,128)(2,1)} %bitcast.5, s32[8,256]{1,0:T(8,128)} %refs_4_.1, s32[8,256]{1,0:T(8,128)} %refs_5_.1, f32[4]{0:T(128)} %refs_6_.1, s32[1,256]{1,0:T(1,128)} %refs_7_.1), custom_call_target="tpu_custom_call" | custom-call | flops 100000000 | bytes 10000000 | tf_op jit(solution)/shard_map/pallas_call | solution.py:509
  116.4 3.0 %copy.10 = f32[4,64,8,256]{3,2,1,0:T(8,128)} copy(f32[4,64,8,256]{3,2,1,0:T(8,128)} %bitcast.4) | data formatting | bytes 4194304
where the time goes:
time: 120 us; the launch traced here: 119 us
  Pallas kernels  116 us (97%)
  local copies, waits for them, and re-layouts  3.05 us (3%)
    pallas_call x1, Pallas kernels, per_device(): pl.pallas_call(body, out_shape=jax.ShapeDtypeStruct((state, LON), F32), i...  116 us
    unnamed x1, local copies, waits for them, and re-layouts  3.05 us

commit v1 on v0

v1 whole, which is shorter than its diff:
```python
import functools

import jax
import jax.numpy as jnp
from jax import lax
from jax.experimental import pallas as pl
from jax.experimental.pallas import tpu as pltpu
from jax.sharding import PartitionSpec as P

F = 4
LEV = 64
ROWS = 8
LON = 256
NB = 8
SLOTS = 32
PLANE = LEV * ROWS
SIZE = {"y": 2, "x": 4, "z": 4}
ORDERS = (("x", "z", "y"), ("z", "y", "x"), ("y", "x", "z"))
GROUPS = 2
DEPTH = LEV // GROUPS
CHUNKS = tuple((order, step, at, rows) for step in range(2) for order, at, rows in (
    (0, 0, 16), (1, 16, 16), (2, 64, 32), (0, 32, 16), (1, 96, 32), (2, 48, 16)))
MESH = pl.DeviceIdType.MESH
BF = jnp.bfloat16
F32 = jnp.float32
NT = (((1,), (1,)), ((), ()))
TN = (((0,), (0,)), ((), ()))


def coords(tile):
    return {"y": tile // 16, "x": (tile // 4) % 4, "z": tile % 4}


def tile_of(at):
    return at["y"] * 16 + at["x"] * 4 + at["z"]


def moved(at, axis, by):
    other = dict(at)
    other[axis] = lax.rem(at[axis] + by, SIZE[axis])
    return other


def rows_of(level):
    return pl.ds(pl.multiple_of(level * ROWS, ROWS), ROWS)


def wide(ref, *at):
    return jnp.concatenate([ref[(0, *at)], ref[(1, *at)]], 1)


def put(ref, value, *at):
    ref[(0, *at)] = value[:, :128]
    ref[(1, *at)] = value[:, 128:]


def kernel(adj, kappa, diff, store, mask, remap, gain, sources, out, *scratch):
    (store_v, st, mx, kap, inv, low, up, vel, diff_v, mask_v, remap_v, coef, dedge, cpl, slots, table,
     s1, r1, r2, s3, r3, surf_s, surf_r, ew_s, ew_r, zw_s, zw_r, mr_s, mr_r, vr_s, vr_r,
     load_sem, top_sem, out_sem, own_sem, e_send, e_recv, h_send, h_recv) = scratch
    tile = lax.axis_index("tile")
    sec = lax.axis_index("sec")
    me = coords(tile)

    def load_half(half, sem):
        part = pl.ds(half * 2 * LEV, 2 * LEV)
        return pltpu.make_async_copy(store.at[:, part], store_v[half], load_sem.at[sem])

    def load_state(g, h):
        return pltpu.make_async_copy(
            adj.at[:, pl.ds(g * DEPTH * ROWS, DEPTH * ROWS), pl.ds(h * 128, 128)], st[g].at[h],
            load_sem.at[8 + 2 * g + h])

    tops = [pltpu.make_async_copy(adj.at[f, pl.ds(0, ROWS)], surf_s[0].at[pl.ds(f * ROWS, ROWS)],
                                  top_sem.at[f]) for f in range(F)]
    for top in tops:
        top.start()
    loads = [
        load_half(0, 0),
        *(load_state(g, h) for g in range(GROUPS) for h in range(2)),
        pltpu.make_async_copy(kappa, kap.at[pl.ds(0, PLANE - ROWS)], load_sem.at[3]),
        pltpu.make_async_copy(diff, diff_v, load_sem.at[4]),
        pltpu.make_async_copy(mask, mask_v, load_sem.at[5]),
        pltpu.make_async_copy(remap, remap_v, load_sem.at[6]),
        load_half(1, 7),
    ]
    for load in loads:
        load.start()

    barrier = pltpu.get_barrier_semaphore()
    greeted = 0
    for axis in ("x", "z", "y"):
        for by in range(1, SIZE[axis]):
            pl.semaphore_signal(barrier, inc=1, device_id={"tile": tile_of(moved(me, axis, by))},
                                device_id_type=MESH)
            greeted += 1
    for by in (1, 31):
        pl.semaphore_signal(barrier, inc=1, device_id={"tile": lax.rem(tile + by, 32)},
                            device_id_type=MESH)
        greeted += 1
    for by in (1, 2, 3):
        pl.semaphore_signal(barrier, inc=1, device_id={"sec": lax.rem(sec + by, 4)},
                            device_id_type=MESH)
        greeted += 1

    def find_slots(reader, _):
        first = jnp.int32(0)
        second = jnp.int32(0)
        for j in range(NB):
            source = sources[0, reader * NB + j]
            second = jnp.where(source // SLOTS == tile, source % SLOTS, second)
            source = sources[0, reader * NB + NB - 1 - j]
            first = jnp.where(source // SLOTS == tile, source % SLOTS, first)
        slots[2 * reader] = first
        slots[2 * reader + 1] = second
        return 0

    lax.fori_loop(0, 32, find_slots, 0)
    pl.semaphore_wait(barrier, greeted)

    def find_blocks():
        for order in range(3):
            axis = ORDERS[order][2]
            for by in range(SIZE[axis]):
                reader = tile_of(moved(me, axis, by))
                holders = [sources[0, reader * NB + j] // SLOTS for j in range(NB)]
                for j in range(NB):
                    rank = jnp.int32(0)
                    for i in range(j):
                        rank = rank + jnp.where(holders[i] == holders[j], 1, 0)
                    table[(order * 4 + by) * NB + j] = holders[j] * 2 + jnp.minimum(rank, 1)

    pending = []
    arrivals = {}
    arrivals_sent = {}

    def send(key, src, dst, send_sem, recv_sem, device):
        copy = pltpu.make_async_remote_copy(src, dst, send_sem, recv_sem, device_id=device,
                                            device_id_type=MESH)
        copy.start()
        pending.append(copy)
        arrivals.setdefault(key, []).append(copy)
        arrivals_sent.setdefault(key, []).append(copy)

    def arrived(key):
        for copy in arrivals.pop(key):
            copy.wait_recv()

    hsem = [0]

    def small(key, src, dst, device):
        n = hsem[0]
        hsem[0] += 1
        send(key, src, dst, h_send.at[n], h_recv.at[n], device)

    def to_sections(key, src, dst):
        for by in (1, 2, 3):
            small(key, src, dst.at[sec], {"sec": lax.rem(sec + by, 4)})

    def to_north_south(key, src, dst):
        small(key, src.at[0], dst.at[0], {"tile": lax.rem(tile + 31, 32)})
        small(key, src.at[1], dst.at[1], {"tile": lax.rem(tile + 1, 32)})

    def sent(key):
        for copy in arrivals_sent.pop(key):
            copy.wait_send()
            pending[:] = [other for other in pending if other is not copy]

    def esem(chunk, stage, by):
        return (chunk * 3 + stage) * 3 + by - 1

    def stage_one(chunk):
        order, half, at, rows = CHUNKS[chunk]
        a1, a2, a3 = ORDERS[order]
        n1, n2, n3 = SIZE[a1], SIZE[a2], SIZE[a3]
        sbuf, rbuf = s1[chunk], r1[chunk]
        for by in list(range(1, n1)) + [0]:
            c1 = lax.rem(me[a1] + by, n1)

            def one_reader(i, _):
                c2, c3 = i // n3, lax.rem(i, n3)
                reader = tile_of({a1: c1, a2: c2, a3: c3})
                for k in range(2):
                    slot = slots[2 * reader + k]
                    block = store_v[half][slot, at:at + rows, :]
                    if by:
                        sbuf[by - 1, c2, c3, k] = block
                    else:
                        rbuf[c2, me[a1], c3, k] = block
                return 0

            lax.fori_loop(0, n2 * n3, one_reader, 0)
            if by:
                n = esem(chunk, 0, by)
                send((chunk, 1), sbuf.at[by - 1], rbuf.at[:, me[a1]], e_send.at[n], e_recv.at[n],
                     {"tile": tile_of(moved(me, a1, by))})

    def stage_two(chunk):
        a1, a2, a3 = ORDERS[CHUNKS[chunk][0]]
        src, dst = r1[chunk], r2[chunk]
        arrived((chunk, 1))
        for by in range(1, SIZE[a2]):
            c2 = lax.rem(me[a2] + by, SIZE[a2])
            n = esem(chunk, 1, by)
            send((chunk, 2), src.at[c2], dst.at[me[a2]], e_send.at[n], e_recv.at[n],
                 {"tile": tile_of(moved(me, a2, by))})
        own = pltpu.make_async_copy(src.at[me[a2]], dst.at[me[a2]], own_sem.at[chunk])
        own.start()
        arrivals[("own", chunk)] = [own]

    def stage_three(chunk):
        order = CHUNKS[chunk][0]
        a1, a2, a3 = ORDERS[order]
        n3 = SIZE[a3]
        src, sbuf, rbuf = r2[chunk], s3[chunk], r3[chunk]
        arrivals.pop(("own", chunk))[0].wait()
        arrived((chunk, 2))
        for by in list(range(1, n3)) + [0]:
            target = moved(me, a3, by)
            reader = tile_of(target)
            for j in range(NB):
                known = table[(order * 4 + by) * NB + j]
                holder = coords(known // 2)
                block = src[holder[a2], holder[a1], target[a3], known % 2]
                if by:
                    sbuf[by - 1, j] = block
                else:
                    rbuf[me[a3], j] = block
            if by:
                n = esem(chunk, 2, by)
                send((chunk, 3), sbuf.at[by - 1], rbuf.at[me[a3]], e_send.at[n], e_recv.at[n],
                     {"tile": reader})

    def assemble(chunk):
        order, half, at, rows = CHUNKS[chunk]
        a3 = ORDERS[order][2]
        arrived((chunk, 3))
        for j in range(NB):
            holder = coords(table[order * 4 * NB + j] // 2)
            block = r3[chunk][holder[a3], j]
            vel[at // LEV, pl.ds(j * LEV + at % LEV, rows), :] = block
            if j in (0, NB - 1) and at >= LEV:
                vr_s[half * GROUPS + (at - LEV) // DEPTH][j // (NB - 1)] = block

    lane = lax.broadcasted_iota(jnp.int32, (ROWS, LON), 1)
    row = lax.broadcasted_iota(jnp.int32, (ROWS, LON), 0)

    def edge_pick(low_lane, high_lane, field=None):
        wanted = jnp.where(row % 2 == 0, low_lane, high_lane)
        pick = lane == wanted
        if field is not None:
            pick = pick & (row // 2 == field)
        return jnp.where(pick, 1.0, 0.0)

    def send_surface(step):
        for f in range(F):
            if step:
                surf_s[step][pl.ds(f * ROWS, ROWS), :] = wide(st[0], f, pl.ds(0, ROWS))
            else:
                tops[f].wait()
        to_sections(("surf", step), surf_s[step], surf_r[step])

    def prepare():
        kap[pl.ds(PLANE - ROWS, ROWS), :] = jnp.zeros((ROWS, LON), F32)

        def level(l, carry):
            g, below = carry
            at = rows_of(l)
            above = kap[at, :]
            p = 1.0 + below * g
            w = 1.0 / (p + above)
            inv[at, :] = w
            low[at, :] = below * w
            up[at, :] = above * w
            return p * w, above

        zero = jnp.zeros((ROWS, LON), F32)
        lax.fori_loop(0, LEV, level, (zero, zero))
        d = diff_v[...]
        is_ocean = sec == 0
        sea = jnp.where(is_ocean, mask_v[...].astype(F32), 1.0)
        east_ok = jnp.where(is_ocean | (lane != 0), 1.0, 0.0)
        west_ok = jnp.where(is_ocean | (lane != LON - 1), 1.0, 0.0)
        north_ok = jnp.where(row != 0, 1.0, 0.0)
        south_ok = jnp.where(row != ROWS - 1, 1.0, 0.0)
        values = (
            pltpu.roll(d, 1, 1) * east_ok, 0.5 * east_ok,
            pltpu.roll(d, LON - 1, 1) * west_ok, 0.5 * west_ok,
            pltpu.roll(d, 1, 0) * north_ok, pltpu.roll(d, ROWS - 1, 0) * south_ok,
            1.0 - 4.0 * d, sea,
        )
        for i, value in enumerate(values):
            for r in range(ROWS):
                coef[i, r] = jnp.broadcast_to(value[r:r + 1], (8, LON))
        tiled = jnp.broadcast_to(d[:, None], (ROWS, DEPTH, LON)).reshape(ROWS * DEPTH, LON)
        dedge[...] = lax.dot_general(edge_pick(LON - 1, 0), tiled, NT,
                                     precision=lax.Precision.HIGHEST, preferred_element_type=F32)

    def couple(step):
        surf_r[step][sec] = surf_s[step][...]
        arrived(("surf", step))
        iota = lax.broadcasted_iota(jnp.int32, (128, LON), 0)

        def parts_of(r):
            cell = remap_v[r:r + 1, :]
            onehot = jnp.where(iota == (cell & 127), 1.0, 0.0).astype(BF)
            high = ((cell >> 11) << 4) + (((cell >> 7) & 1) << 3) + ((cell >> 8) & 7)
            return onehot, high, mask_v[r:r + 1, :].astype(F32)

        @pl.when(sec == 0)
        def _():
            table = jnp.concatenate(
                [surf_r[step][s + 1, f * ROWS:(f + 1) * ROWS, h * 128:(h + 1) * 128]
                 for f in range(F) for s in range(3) for h in range(2)], 0).astype(BF)
            iota48 = lax.broadcasted_iota(jnp.int32, (48, LON), 0)
            for r in range(ROWS):
                onehot, high, sea = parts_of(r)
                found = jnp.dot(table, onehot, preferred_element_type=F32)
                hit = iota48 == high
                for f in range(F):
                    value = jnp.sum(jnp.where(hit, found[f * 48:(f + 1) * 48], 0.0), 0, keepdims=True)
                    cpl[f * ROWS + r:f * ROWS + r + 1, :] = gain[f] * sea * value

        @pl.when(sec != 0)
        def _():
            iota16 = lax.broadcasted_iota(jnp.int32, (16, LON), 0)
            total = jnp.zeros((F * 16, 128), F32)
            for r in range(ROWS):
                onehot, high, sea = parts_of(r)
                hit = iota16 == high - (sec - 1) * 16
                spread = []
                for f in range(F):
                    value = gain[f] * sea * surf_r[step][0, f * ROWS + r:f * ROWS + r + 1, :]
                    spread.append(jnp.where(hit, value, 0.0))
                spread = jnp.concatenate(spread, 0).astype(BF)
                total = total + lax.dot_general(spread, onehot, NT, preferred_element_type=F32)
            for f in range(F):
                for h in range(2):
                    at = (f * 2 + h) * ROWS
                    cpl[f * ROWS:(f + 1) * ROWS, h * 128:(h + 1) * 128] = total[at:at + ROWS]

        for f in range(F):
            at = f, pl.ds(0, ROWS)
            put(st[0], wide(st[0], *at) + cpl[pl.ds(f * ROWS, ROWS), :], *at)

    def eliminate(g):
        def forward(i, carry):
            at = rows_of(g * DEPTH + i)
            w, a = inv[at, :], low[at, :]
            result = []
            for f in range(F):
                d = wide(st[g], f, rows_of(i)) * w + a * carry[f]
                put(st[g], d, f, rows_of(i))
                result.append(d)
            return tuple(result)

        start = tuple(wide(st[g - 1], f, rows_of(DEPTH - 1)) if g else jnp.zeros((ROWS, LON), F32)
                      for f in range(F))
        lax.fori_loop(0, DEPTH, forward, start)

    def substitute():
        later = tuple(jnp.zeros((ROWS, LON), F32) for _ in range(F))
        for g in reversed(range(GROUPS)):
            def backward(i, carry):
                i = DEPTH - 1 - i
                l = g * DEPTH + i
                e = up[rows_of(l), :]
                result = []
                for f in range(F):
                    x = wide(st[g], f, rows_of(i)) + e * carry[f]
                    put(mx, x, pl.ds(f * PLANE + l, ROWS, stride=LEV))
                    result.append(x)
                return tuple(result)

            later = lax.fori_loop(0, DEPTH, backward, later)

    def send_mixed(step):
        for side, edge in ((0, 0), (1, ROWS - 1)):
            for f in range(F):
                mr_s[step][side, f * LEV:(f + 1) * LEV, :] = wide(
                    mx, pl.ds(f * PLANE + edge * LEV, LEV)).astype(BF)
        to_north_south(("mr", step), mr_s[step], mr_r[step])
        for g in range(GROUPS):
            total = jnp.zeros((ROWS, ROWS * DEPTH), F32)
            for f in range(F):
                rows = jnp.concatenate(
                    [wide(mx, pl.ds(f * PLANE + r * LEV + g * DEPTH, DEPTH)) for r in range(ROWS)], 0)
                total = total + lax.dot_general(edge_pick(0, LON - 1, f).astype(BF), rows.astype(BF), NT,
                                                preferred_element_type=F32)
            ew_s[step][g] = total
        to_sections(("ew", step), ew_s[step], ew_r[step])

    def send_velocity(step, g):
        n = step * GROUPS + g
        to_north_south(("vr", n), vr_s[n], vr_r[n])
        rows = jnp.concatenate([vel[0, pl.ds(r * LEV + g * DEPTH, DEPTH), :] for r in range(ROWS)], 0)
        zw_s[n][...] = lax.dot_general(edge_pick(0, LON - 1).astype(BF), rows, NT,
                                       preferred_element_type=F32)
        to_sections(("zw", n), zw_s[n], zw_r[n])

    def stencil(g):
        def tile16(i, _):
            rel = i * 16
            at = g * DEPTH + rel
            for part in range(2):
                lo = at + part * 8
                south = [None] * F
                open_sum = [None] * F
                for r in range(ROWS):
                    here = pl.ds(pl.multiple_of(r * LEV + at, 16), 16)
                    z = vel[0, here, :].astype(F32)[part * 8:part * 8 + 8]
                    v = 0.5 * vel[1, here, :].astype(F32)[part * 8:part * 8 + 8]
                    c_e = coef[0, r] + coef[1, r] * z
                    c_w = coef[2, r] - coef[3, r] * z
                    c_n = coef[4, r] + v
                    c_s = coef[5, r] - v
                    for f in range(F):
                        m = wide(mx, pl.ds(pl.multiple_of(f * PLANE + r * LEV + lo, 8), 8))
                        total = m * coef[6, r]
                        total = total + pltpu.roll(m * c_e, LON - 1, 1)
                        total = total + pltpu.roll(m * c_w, 1, 1)
                        if r:
                            total = total + south[f]
                            put(st[g], (open_sum[f] + m * c_n) * coef[7, r - 1],
                                f, pl.ds((rel + part * 8) * ROWS + r - 1, 8, stride=ROWS))
                        south[f] = m * c_s
                        open_sum[f] = total
                for f in range(F):
                    put(st[g], open_sum[f] * coef[7, ROWS - 1],
                        f, pl.ds((rel + part * 8) * ROWS + ROWS - 1, 8, stride=ROWS))
            return 0

        lax.fori_loop(0, DEPTH // 16, tile16, 0)

    def add_halos(step, g):
        n = step * GROUPS + g
        if g == 0:
            arrived(("mr", step))
            arrived(("ew", step))
        arrived(("vr", n))
        arrived(("zw", n))
        even = lax.broadcasted_iota(jnp.int32, (ROWS, ROWS * DEPTH), 0) % 2 == 0
        east = jnp.where(sec == 0, 1, jnp.where(sec == 3, 1, sec + 1))
        west = jnp.where(sec == 0, 2, jnp.where(sec == 1, 3, sec - 1))
        m = jnp.where(even, ew_r[step][east, g], ew_r[step][west, g])
        z = jnp.where(even, zw_r[n][east], -zw_r[n][west])
        value = jnp.where(sec == 0, 0.0, m * (dedge[...] + 0.5 * z)).astype(BF)
        for f in range(F):
            for side, edge, missing, sign in ((0, ROWS - 1, 31, 0.5), (1, 0, 0, -0.5)):
                rows = mr_r[step][side, f * LEV + g * DEPTH:f * LEV + (g + 1) * DEPTH, :].astype(F32)
                v = vr_r[n][side].astype(F32)
                sea = jnp.where(tile == missing, 0.0, coef[7, edge, 0:1, :])
                term = rows * (diff_v[edge:edge + 1, :] + sign * v) * sea
                at = f, pl.ds(edge, DEPTH, stride=ROWS)
                put(st[g], wide(st[g], *at) + term, *at)

            @pl.when(sec != 0)
            def _():
                place = edge_pick(LON - 1, 0, f).astype(BF)
                add = lax.dot_general(value, place, TN, preferred_element_type=F32)
                for r in range(ROWS):
                    at = f, pl.ds(r, DEPTH, stride=ROWS)
                    put(st[g], wide(st[g], *at) + add[r * DEPTH:(r + 1) * DEPTH], *at)

            if step:
                at = pl.ds(g * DEPTH * ROWS, DEPTH * ROWS)
                for h in range(2):
                    copy = pltpu.make_async_copy(
                        st[g].at[h, f], out.at[f, at, pl.ds(h * 128, 128)], out_sem.at[g, f, h])
                    copy.start()
                    outs.append(copy)

    stages = {"1": stage_one, "2": stage_two, "3": stage_three, "4": assemble}

    def run(*steps):
        for stage, group in (step.split(".") for step in steps):
            for piece in (2, 1, 0):
                stages[stage](int(group) * 3 + piece)

    outs = []
    send_surface(0)
    loads[0].wait()
    run("1.0", "1.1")
    find_blocks()
    for load in loads[1:]:
        load.wait()
    prepare()
    run("2.0", "1.2")
    couple(0)
    eliminate(0)
    eliminate(1)
    substitute()
    send_mixed(0)
    run("2.1", "3.0", "1.3", "2.2", "3.1", "4.0")
    send_velocity(0, 0)
    stencil(0)
    run("2.3", "3.2", "4.1")
    send_velocity(0, 1)
    stencil(1)
    add_halos(0, 0)
    send_surface(1)
    run("3.3")
    add_halos(0, 1)
    couple(1)
    eliminate(0)
    eliminate(1)
    substitute()
    send_mixed(1)
    run("4.2")
    send_velocity(1, 0)
    stencil(0)
    run("4.3")
    send_velocity(1, 1)
    stencil(1)
    add_halos(1, 0)
    add_halos(1, 1)
    for copy in outs:
        copy.wait()
    for copy in pending:
        copy.wait_send()


def per_device(adjoint, kappa, diffusion, gain, store, sources, ocean_mask, remap):
    vmem, dma = pltpu.VMEM, pltpu.SemaphoreType.DMA
    both = range(2)

    def each(lead, count):
        return [vmem(lead(*(SIZE[a] for a in ORDERS[c[0]])) + (count, c[3], LON), BF) for c in CHUNKS]

    def grouped(shape, kind):
        return [vmem(shape, kind) for _ in range(2 * GROUPS)]

    def twice(shape, kind):
        return [vmem(shape, kind) for _ in both]

    scratch = [
        twice((SLOTS, 2 * LEV, LON), BF), [vmem((2, F, DEPTH * ROWS, 128), F32) for _ in range(GROUPS)],
        vmem((2, F * PLANE, 128), F32),
        vmem((PLANE, LON), F32), vmem((PLANE, LON), F32), vmem((PLANE, LON), F32), vmem((PLANE, LON), F32),
        vmem((2, PLANE, LON), BF), vmem((ROWS, LON), F32), vmem((ROWS, LON), jnp.int32),
        vmem((ROWS, LON), jnp.int32), vmem((8, ROWS, 8, LON), F32), vmem((ROWS, ROWS * DEPTH), F32),
        vmem((F * ROWS, LON), F32), pltpu.SMEM((64,), jnp.int32), pltpu.SMEM((96,), jnp.int32),
        each(lambda n1, n2, n3: (n1 - 1, n2, n3), 2), each(lambda n1, n2, n3: (n2, n1, n3), 2),
        each(lambda n1, n2, n3: (n2, n1, n3), 2), each(lambda n1, n2, n3: (n3 - 1,), NB),
        each(lambda n1, n2, n3: (n3,), NB),
        twice((F * ROWS, LON), F32), twice((4, F * ROWS, LON), F32),
        twice((GROUPS, ROWS, ROWS * DEPTH), F32), twice((4, GROUPS, ROWS, ROWS * DEPTH), F32),
        grouped((ROWS, ROWS * DEPTH), F32), grouped((4, ROWS, ROWS * DEPTH), F32),
        twice((2, F * LEV, LON), BF), twice((2, F * LEV, LON), BF),
        grouped((2, DEPTH, LON), BF), grouped((2, DEPTH, LON), BF),
        dma((12,)), dma((F,)), dma((GROUPS, F, 2)), dma((len(CHUNKS),)), dma((9 * len(CHUNKS),)), dma((9 * len(CHUNKS),)), dma((36,)), dma((36,)),
    ]
    leaves, tree = jax.tree.flatten(scratch)

    def body(*refs):
        head, rest = refs[:9], refs[9:]
        kernel(*head, *jax.tree.unflatten(tree, rest))

    anywhere = pl.BlockSpec(memory_space=pl.ANY)
    scalar = pl.BlockSpec(memory_space=pltpu.SMEM)
    result = pl.pallas_call(
        body,
        out_shape=jax.ShapeDtypeStruct((F, PLANE, LON), F32),
        in_specs=[anywhere] * 6 + [scalar] * 2,
        out_specs=anywhere,
        scratch_shapes=leaves,
        compiler_params=pltpu.CompilerParams(
            collective_id=0, has_side_effects=True, vmem_limit_bytes=56 * 2**20
        ),
        cost_estimate=pl.CostEstimate(flops=100_000_000, bytes_accessed=10_000_000, transcendentals=0),
    )(
        adjoint.reshape(F, PLANE, LON), kappa.reshape(PLANE - ROWS, LON), diffusion,
        store.reshape(SLOTS, F * LEV, LON), ocean_mask, remap, gain, sources,
    )
    return result.reshape(F, LEV, ROWS, LON)


def solution(mesh):
    return jax.shard_map(
        per_device,
        mesh=mesh,
        in_specs=(
            P(None, None, "tile", "sec"),
            P(None, "tile", "sec"),
            P("tile", "sec"),
            P(),
            P("sec", "tile", None, None, None),
            P("sec", None),
            P("tile", None),
            P("tile", None),
        ),
        out_specs=P(None, None, "tile", "sec"),
        check_vma=False,
    )
```

time: 120 us -> 108 us (0.900)
  Pallas kernels: 116 us -> 105 us
    pallas_call x1, Pallas kernels: 116 us -> 105 us  [per_device(): pl.pallas_call(body, out_shape=jax.ShapeDtypeStruct((F, PLANE, LON), F32)...]
where the time goes in v1:
time: 108 us
  Pallas kernels  105 us (97%)
  local copies, waits for them, and re-layouts  3.05 us (3%)
    pallas_call x1, Pallas kernels, per_device(): pl.pallas_call(body, out_shape=jax.ShapeDtypeStruct((F, PLANE, LON), F32)...  105 us
    unnamed x1, local copies, waits for them, and re-layouts  3.05 us

profile of v1, /device:TPU:1, one launch (start us, length us, event | category | flops | bytes accessed | tf_op | source)
XLA Modules:
  0.0 107.6 jit_solution(6531541540650869788)
XLA Ops:
  0.0 104.6 %shard_map.82 = f32[4,512,256]{2,1,0:T(8,128)} custom-call(f32[4,512,256]{2,1,0:T(8,128)} %bitcast.6, f32[504,256]{1,0:T(8,128)} %bitcast.7, f32[8,256]{1,0:T(8,128)} %refs_2_.1, bf16[32,256,256]{2,1,0:T(8,128)(2,1)} %bitcast.5, s32[8,256]{1,0:T(8,128)} %refs_4_.1, s32[8,256]{1,0:T(8,128)} %refs_5_.1, f32[4]{0:T(128)} %refs_6_.1, s32[1,256]{1,0:T(1,128)} %refs_7_.1), custom_call_target="tpu_custom_call" | custom-call | flops 100000000 | bytes 10000000 | tf_op jit(solution)/shard_map/pallas_call | solution.py:561
  104.6 3.0 %copy.10 = f32[4,64,8,256]{3,2,1,0:T(8,128)} copy(f32[4,64,8,256]{3,2,1,0:T(8,128)} %bitcast.4) | data formatting | bytes 4194304

commit v2 on v1

--- a/solution.py
+++ b/solution.py
@@ -356,7 +356,7 @@
 
         start = tuple(wide(st[g - 1], f, rows_of(DEPTH - 1)) if g else jnp.zeros((ROWS, LON), F32)
                       for f in range(F))
-        lax.fori_loop(0, DEPTH, forward, start)
+        lax.fori_loop(0, DEPTH, forward, start, unroll=4)
 
     def substitute():
         later = tuple(jnp.zeros((ROWS, LON), F32) for _ in range(F))
@@ -372,7 +372,7 @@
                     result.append(x)
                 return tuple(result)
 
-            later = lax.fori_loop(0, DEPTH, backward, later)
+            later = lax.fori_loop(0, DEPTH, backward, later, unroll=4)
 
     def send_mixed(step):
         for side, edge in ((0, 0), (1, ROWS - 1)):

time: 108 us -> 107 us (level)
  no operation moved by 1% of the time
where the time goes in v2:
time: 107 us
  Pallas kernels  104 us (97%)
  local copies, waits for them, and re-layouts  3.05 us (3%)
    pallas_call x1, Pallas kernels, per_device(): pl.pallas_call(body, out_shape=jax.ShapeDtypeStruct((F, PLANE, LON), F32)...  104 us
    unnamed x1, local copies, waits for them, and re-layouts  3.05 us

profile of v2, /device:TPU:1, one launch (start us, length us, event | category | flops | bytes accessed | tf_op | source)
XLA Modules:
  0.0 107.2 jit_solution(8138040281883304102)
XLA Ops:
  0.0 104.1 %shard_map.82 = f32[4,512,256]{2,1,0:T(8,128)} custom-call(f32[4,512,256]{2,1,0:T(8,128)} %bitcast.6, f32[504,256]{1,0:T(8,128)} %bitcast.7, f32[8,256]{1,0:T(8,128)} %refs_2_.1, bf16[32,256,256]{2,1,0:T(8,128)(2,1)} %bitcast.5, s32[8,256]{1,0:T(8,128)} %refs_4_.1, s32[8,256]{1,0:T(8,128)} %refs_5_.1, f32[4]{0:T(128)} %refs_6_.1, s32[1,256]{1,0:T(1,128)} %refs_7_.1), custom_call_target="tpu_custom_call" | custom-call | flops 100000000 | bytes 10000000 | tf_op jit(solution)/shard_map/pallas_call | solution.py:561
  104.1 3.0 %copy.10 = f32[4,64,8,256]{3,2,1,0:T(8,128)} copy(f32[4,64,8,256]{3,2,1,0:T(8,128)} %bitcast.4) | data formatting | bytes 4194304
